TPU v7x, 512 devices: a whole 4x8x8 slice. The times are simulated.
512 devices in a mesh: row: 32 (over y_lo, z), col: 16 (over x, y_hi, core).
Axes of the slice: x: 4, y: 8 (y_hi: 2, y_lo: 4; y = y_hi * 4 + y_lo), z: 8, core: 2. Of those that a mesh axis runs over, the one named last changes fastest.
Arguments:
- grad_out: bfloat16 [65536, 256], P(('row', 'col')), may hold values from -6 to 6
- relu_mask: int32 [65536, 256], P(('row', 'col')), may hold values 0 or 1
- features: bfloat16 [16, 4096, 256], P('col', 'row'), may hold values from -0.119628906 to 0.119628906
- weight: bfloat16 [256, 256], replicated, may hold values from -0.375 to 0.375
- tile_values: bfloat16 [32, 16, 144, 128, 128], P('row', 'col'), may hold values from 0.0049743652 to 0.049804688
- tile_lists: int32 [32, 16, 3, 144], P('row', 'col'), may hold values from 0 to 511, as said below
- tile_count: int32 [32, 16], P('row', 'col'), may hold values from 18 to 144, as said below
Outputs:
- grad_input: bfloat16 [16, 4096, 256], P('col', 'row')
- grad_weight: float32 [256, 256], replicated
Inputs may be any that keep to these rules, and one draw needn't show every extreme that they name: `tile_lists`: for device (r, c) the first tile_count[r, c] entries name distinct tiles with block row in r * 16 to (r + 1) * 16 - 1 and block column in c * 32 to (c + 1) * 32 - 1; row 2 of each device's list holds each slot 0 to 143 once; entries past the count lie in the same ranges and are ignored. `tile_count`: some device holds exactly 144 live entries.
All inputs are finite; a program needn't handle non-finite values. No bound on the sum of `relu_mask` on one device may be relied on, other than what follows from the above.
Results may differ from a plain program's by a relative error of at most 0.0049.
Values may be sent and summed in bfloat16 or wider, within the bound.
A program may use at most 128 MiB of HBM per device.

v0:
```python
import jax
import jax.numpy as jnp
from jax import lax
from jax.sharding import PartitionSpec as P


def body(grad_out, relu_mask, features, weight, tile_values, tile_lists, tile_count):
    dz = grad_out * relu_mask.astype(jnp.bfloat16)
    gathered = lax.all_gather(dz, "col", axis=0, tiled=True)
    block = tile_values.shape[-1]
    width = dz.shape[1]
    capacity = tile_values.shape[2]
    rows_blocks = gathered.shape[0] // block
    cols_blocks = rows_blocks * lax.axis_size("row") // lax.axis_size("col")
    row_id = lax.axis_index("row")
    col_id = lax.axis_index("col")
    lists = tile_lists[0, 0]
    entries = jnp.arange(capacity, dtype=jnp.int32)
    inverse = jnp.zeros((capacity,), jnp.int32).at[lists[2]].set(entries)
    block_rows = lists[0][inverse] - row_id * rows_blocks
    block_cols = lists[1][inverse] - col_id * cols_blocks
    live = inverse < tile_count[0, 0]
    blocks = gathered.reshape(rows_blocks, block, width)[block_rows]
    prods = jnp.einsum(
        "tik,tid->tkd", tile_values[0, 0], blocks, preferred_element_type=jnp.float32
    )
    inside = live & (block_cols >= 0) & (block_cols < cols_blocks)
    targets = jnp.where(inside, block_cols, cols_blocks)
    summed = jnp.zeros((cols_blocks, block, width), jnp.float32).at[targets].add(prods, mode="drop")
    partial_sum = summed.reshape(cols_blocks * block, width)
    column_part = lax.psum_scatter(partial_sum, "row", scatter_dimension=0, tiled=True)
    agg_b = column_part.astype(jnp.bfloat16)
    grad_rows = lax.dot_general(
        agg_b, weight, (((1,), (1,)), ((), ())), preferred_element_type=jnp.float32
    )
    weight_term = lax.dot_general(
        features[0], agg_b, (((0,), (0,)), ((), ())), preferred_element_type=jnp.float32
    )
    grad_weight = lax.psum(weight_term, ("row", "col"))
    return (grad_rows.astype(jnp.bfloat16)[None], grad_weight)


def solution(mesh):
    return jax.shard_map(
        body,
        mesh=mesh,
        in_specs=(
            P(("row", "col"), None),
            P(("row", "col"), None),
            P("col", "row", None),
            P(),
            P("row", "col", None, None, None),
            P("row", "col", None, None),
            P("row", "col"),
        ),
        out_specs=(P("col", "row", None), P()),
        check_vma=False,
    )
```

profile of v0, /device:TPU:1, one launch (start us, length us, event | category | flops | bytes accessed | tf_op | source)
XLA Modules:
  0.0 602.2 jit_solution(16494548598807936647)
XLA Ops:
  7.2 0.0 copy-start
  7.2 0.0 all-gather.2.cloned.1.call-start
  7.2 1.6 convert_multiply_fusion
  8.8 0.0 all-gather.2.cloned.1.call-update
  8.9 0.0 reduce-scatter.2.cloned.1.call-start
  9.6 0.7 compare_select_fusion.1
  10.2 1.0 scatter_custom_fusion
  11.3 0.7 fusion.7
  12.0 1.6 gather_fusion
  13.6 1.6 gather_fusion.1
  15.3 61.9 %all-gather.2.cloned.1.call-done = bf16[2048,256]{1,0:T(8,128)(2,1)} async-done(((bf16[128,256]{1,0:T(8,128)(2,1)}), bf16[2048,256]{1,0:T(8,128)(2,1)}) %all-gather.2.cloned.1.call-update) | async-done | bytes 1048592 | tf_op jit(solution)/shard_map/all_gather | solution.py:9
  77.2 8.5 %gather_fusion.2 = bf16[144,128,256]{2,1,0:T(8,128)(2,1)} fusion(bf16[16,128,256]{2,1,0:T(8,128)(2,1)} %bitcast.28, s32[1024]{0:T(1024)S(1)} %pad_clamp_fusion), kind=kCustom, calls=%fused_computation.2 | custom fusion | bytes 18874944 | tf_op jit(solution)/shard_map/gather | solution.py:23
  85.7 11.9 %convolution_bitcast_fusion = f32[144,128,256]{1,2,0:T(8,128)} fusion(bf16[144,128,256]{2,1,0:T(8,128)(2,1)} %gather_fusion.2, bf16[1,1,144,128,128]{4,3,2,1,0:T(8,128)(2,1)} %param.11), kind=kOutput, calls=%fused_computation.5 | convolution fusion | flops 1207959552 | bytes 33030144 | tf_op jit(solution)/shard_map/tik,tid->tkd/dot_general | solution.py:24
  97.5 18.6 %copy.12 = f32[144,128,256]{2,1,0:T(8,128)} copy(f32[144,128,256]{1,2,0:T(8,128)} %convolution_bitcast_fusion) | data formatting | bytes 37748736 | tf_op jit(solution)/shard_map/tik,tid->tkd/dot_general | solution.py:24
  116.2 2.5 broadcast_in_dim.17
  118.7 0.0 copy-start.1
  118.7 40.8 %scatter_fusion = f32[32,128,256]{2,1,0:T(8,128)} fusion(f32[32,128,256]{2,1,0:T(8,128)} %broadcast_in_dim.17, s32[144]{0:T(256)S(1)} %compare_select_fusion.2, f32[144,128,256]{2,1,0:T(8,128)} %copy.12), kind=kCustom, calls=%fused_computation.4 | custom fusion | flops 4718592 | bytes 56623680 | tf_op jit(solution)/shard_map/scatter-add | solution.py:29
  159.5 0.0 reduce-scatter.2.cloned.1.call-update
  159.5 0.0 all-reduce.2.cloned.1.call-start
  159.6 144.6 %reduce-scatter.2.cloned.1.call-done = f32[128,256]{1,0:T(8,128)} async-done(((f32[4096,256]{1,0:T(8,128)}), f32[128,256]{1,0:T(8,128)}) %reduce-scatter.2.cloned.1.call-update) | async-done | bytes 131088 | tf_op jit(solution)/shard_map/reduce_scatter | solution.py:31
  304.1 0.0 copy-done.1
  304.1 1.8 convolution_bitcast_fusion.1
  305.9 0.0 all-reduce.2.cloned.1.call-update
  306.0 0.0 copy-done
  306.0 1.7 fusion.1
  307.7 286.2 %all-reduce.2.cloned.1.call-done = f32[256,256]{0,1:T(8,128)} async-done(((f32[256,256]{0,1:T(8,128)}), f32[256,256]{0,1:T(8,128)}) %all-reduce.2.cloned.1.call-update) | async-done | bytes 262160 | tf_op jit(solution)/shard_map/psum | solution.py:39
  593.9 1.8 copy.13
  (7 shorter events, 0.0 us)
Async XLA Ops:
  7.2 298.8 %copy-start = (bf16[256,256]{1,0:T(8,128)(2,1)S(1)}, bf16[256,256]{1,0:T(8,128)(2,1)}, u32[]{:S(2)}) copy-start(bf16[256,256]{1,0:T(8,128)(2,1)} %param.10) | copy-start | bytes 393220
  7.2 70.0 %all-gather.2.cloned.1.call-start = ((), (), s32[]{:S(2)}) async-start(), calls=%async_computation.1 | async-start | bytes 1114112 | tf_op jit(solution)/shard_map/all_gather | solution.py:9
  8.9 295.3 %reduce-scatter.2.cloned.1.call-start = ((), (), s32[]{:S(2)}) async-start(), calls=%async_computation.2 | async-start | bytes 4325376 | tf_op jit(solution)/shard_map/reduce_scatter | solution.py:31
  118.7 185.4 %copy-start.1 = (bf16[1,128,256]{2,1,0:T(8,128)(2,1)S(1)}, bf16[1,128,256]{2,1,0:T(8,128)(2,1)}, u32[]{:S(2)}) copy-start(bf16[1,128,256]{2,1,0:T(8,128)(2,1)} %param.9) | copy-start | bytes 196612
  159.5 434.4 %all-reduce.2.cloned.1.call-start = ((), (), s32[]{:S(2)}) async-start(), calls=%async_computation.3 | async-start | bytes 524288 | tf_op jit(solution)/shard_map/psum | solution.py:39
Sparse Core Ops, SparseCore 0:
  11.9 65.3 all-gather.1
  159.6 144.4 reduce-scatter.1
  309.7 284.1 all-reduce.1
where the time goes:
time: 603 us; the launch traced here: 602 us
  waiting for transfers between devices  493 us (82%)
  other arithmetic  43.1 us (7%)
  local copies, waits for them, and re-layouts  36.4 us (6%)
  matrix products  15.4 us (3%)
  between operations  14.5 us (2%)
    psum x1, waiting for transfers between devices, body(): grad_weight = lax.psum(weight_term, ('row', 'col'))  286 us
    reduce_scatter x1, waiting for transfers between devices, body(): lax.psum_scatter(partial_sum, 'row', scatter_dimension=0, tiled=True)  145 us
    all_gather x1, waiting for transfers between devices, body(): gathered = lax.all_gather(dz, 'col', axis=0, tiled=True)  61.9 us
    scatter-add x1, other arithmetic, body(): jnp.zeros((cols_blocks, block, width), jnp.float32).at[targets]  40.8 us
    dot_general x1, local copies, waits for them, and re-layouts, body(): jnp.einsum('tik,tid->tkd', tile_values[0, 0], blocks, preferred_element_t...  18.6 us
  transfers between devices with their start and end apart: 3, of which 3 were waited for; matrix products, arithmetic and copies ran while one was open for 1% of the time, Pallas kernels for 0%

commit v1 on v0

v1 whole, which is shorter than its diff:
```python
import functools

import jax
import jax.numpy as jnp
from jax import lax
from jax.experimental import pallas as pl
from jax.experimental.pallas import tpu as pltpu
from jax.sharding import PartitionSpec as P

NZ, NYL, NX = 8, 4, 4
NG = 8
NY = 8
BLOCK, D = 128, 256
BR, BC, CAP = 16, 32, 144
PIECES = 2
HALF = D // 2
F32, BF16 = jnp.float32, jnp.bfloat16


def kernel(
    go, mask, feat, wgt, tiles, table, gi, gw,
    tiles_v, ag, dzall, w, part, zsend, zrecv, sums, ysend, yrecv,
    w1, r1, s1, r2, s2, r3, f1, f2,
    tile_sem, ag_ss, ag_rs, z_ss, z_rs, y_ss, y_rs, g_ss, g_rs,
):
    row, col = lax.axis_index("row"), lax.axis_index("col")
    ylo, z = row // NZ, row % NZ
    x, yh, core = col // 4, (col // 2) % 2, col % 2
    g = x * 2 + core
    y = yh * NYL + ylo

    def g_peer(q):
        return row, (q // 2) * 4 + yh * 2 + q % 2

    def y_peer(q):
        return (q % NYL) * NZ + z, x * 4 + (q // NYL) * 2 + core

    def z_peer(q):
        return ylo * NZ + q, col

    def remote(src, dst, ssem, rsem, to):
        return pltpu.make_async_remote_copy(
            src_ref=src, dst_ref=dst, send_sem=ssem, recv_sem=rsem,
            device_id=to, device_id_type=pl.DeviceIdType.MESH,
        )

    sent = []

    def start(src, dst, ssem, rsem, to):
        copy = remote(src, dst, ssem, rsem, to)
        copy.start()
        sent.append(copy)

    def arrived(dst, sem, frm):
        remote(dst, dst, sem, sem, frm).wait_recv()

    tile_copies = []
    for i in range(4):
        part_of = pl.ds(i * (CAP // 4), CAP // 4)
        copy = pltpu.make_async_copy(tiles.at[part_of], tiles_v.at[part_of], tile_sem.at[i])
        copy.start()
        tile_copies.append(copy)

    barrier = pltpu.get_barrier_semaphore()
    for o in range(1, 8):
        for to in (g_peer((g + o) % NG), y_peer((y + o) % NY), z_peer((z + o) % NZ)):
            pl.semaphore_signal(barrier, inc=1, device_id=to, device_id_type=pl.DeviceIdType.MESH)
    dz = go[...].astype(F32) * mask[...].astype(F32)
    ag[col] = dz.T.astype(BF16)
    tiles_v[CAP] = jnp.zeros((BLOCK, BLOCK), BF16)
    pl.semaphore_wait(barrier, 21)

    rows = D // PIECES

    def slot_of(xq, yq, cq):
        return xq * 4 + yq * 2 + cq

    def ag_send(slot, p, to_col, k):
        ref = ag.at[slot, pl.ds(p * rows, rows)]
        start(ref, ref, ag_ss.at[k, p], ag_rs.at[slot, p], (row, to_col))

    def ag_wait(slot, p, from_col):
        arrived(ag.at[slot, pl.ds(p * rows, rows)], ag_rs.at[slot, p], (row, from_col))

    xs = [(x + o) % NX for o in (1, 3, 2)]
    for p in range(PIECES):
        ag_send(col, p, slot_of(x, 1 - yh, core), 0)
    for p in range(PIECES):
        for k, xq in enumerate(xs):
            ag_send(col, p, slot_of(xq, yh, core), 1 + k)
    for p in range(PIECES):
        ag_send(col, p, slot_of(x, yh, 1 - core), 4)
    over = slot_of(x, 1 - yh, core)
    for p in range(PIECES):
        ag_wait(over, p, over)
        for k, xq in enumerate(xs):
            ag_send(over, p, slot_of(xq, yh, core), 5 + k)
        ag_send(over, p, slot_of(x, yh, 1 - core), 8)
    for p in range(PIECES):
        for k, xq in enumerate(xs):
            ag_wait(slot_of(xq, yh, core), p, slot_of(xq, yh, core))
            ag_send(slot_of(xq, yh, core), p, slot_of(x, yh, 1 - core), 9 + k)
    for p in range(PIECES):
        for k, xq in enumerate(xs):
            ag_wait(slot_of(xq, 1 - yh, core), p, slot_of(xq, yh, core))
            ag_send(slot_of(xq, 1 - yh, core), p, slot_of(x, yh, 1 - core), 12 + k)
    for xq in range(NX):
        for yq in range(2):
            for p in range(PIECES):
                ag_wait(slot_of(xq, yq, 1 - core), p, slot_of(x, yh, 1 - core))
    for i in range(BR):
        dzall[:, i * BLOCK:(i + 1) * BLOCK] = ag[i]
    for copy in tile_copies:
        copy.wait()

    def compute(zq):
        def pair(h, carry):
            for j in range(2):
                first = ((2 * h + j) * NZ + zq) * BR
                for i in range(BR):
                    w[i * BLOCK:(i + 1) * BLOCK, j * BLOCK:(j + 1) * BLOCK] = tiles_v[table[first + i]]
            res = jnp.dot(dzall[...], w[...], preferred_element_type=F32)
            part[zq, 2 * h] = res[:, :BLOCK]
            part[zq, 2 * h + 1] = res[:, BLOCK:]
            return carry

        lax.fori_loop(0, NYL // 2, pair, 0)

    ways = (z_peer((z + 1) % NZ), z_peer((z + NZ - 1) % NZ))
    order = [(ylo + 1 + k) % NYL for k in range(NYL)]
    compute((z + 4) % NZ)
    for s in range(4):
        if s:
            compute((z + 4 - s) % NZ)
            compute((z + 4 + s) % NZ)
        for k, yq in enumerate(order):
            for d in range(2):
                dest = (z + 4 - s) % NZ if d == 0 else (z + 4 + s) % NZ
                mine = pl.ds(d * HALF, HALF)
                if s == 0:
                    zsend[d, s, yq, mine] = part[dest, yq, mine].astype(BF16)
                    src, dst = zsend.at[d, s, yq, mine], zrecv.at[d, s, yq, mine]
                elif s == 1:
                    arrived(zrecv.at[d, 0, yq, mine], z_rs.at[d, 0, yq], ways[1 - d])
                    other = pl.ds((1 - d) * HALF, HALF)
                    got = part[dest, yq, mine] + zrecv[d, 0, yq, mine].astype(F32)
                    zsend[d, s, yq, mine] = got.astype(BF16)
                    zsend[d, s, yq, other] = part[dest, yq, other].astype(BF16)
                    src, dst = zsend.at[d, s, yq], zrecv.at[d, s, yq]
                else:
                    arrived(zrecv.at[d, s - 1, yq], z_rs.at[d, s - 1, yq], ways[1 - d])
                    got = part[dest, yq] + zrecv[d, s - 1, yq].astype(F32)
                    zsend[d, s, yq] = got.astype(BF16)
                    src, dst = zsend.at[d, s, yq], zrecv.at[d, s, yq]
                start(src, dst, z_ss.at[d, s, yq], z_rs.at[d, s, yq], ways[d])
    compute(z)
    for k, yq in enumerate(order):
        for d in range(2):
            arrived(zrecv.at[d, 3, yq], z_rs.at[d, 3, yq], ways[1 - d])
        total = part[z, yq] + zrecv[0, 3, yq].astype(F32) + zrecv[1, 3, yq].astype(F32)
        if k < 3:
            ysend[yq] = total.astype(BF16)
            start(ysend.at[yq], yrecv.at[ylo], y_ss.at[yq], y_rs.at[ylo], (yq * NZ + z, col))
        else:
            sums[...] = total
    agg = sums[...]
    for yq in order[:3]:
        arrived(yrecv.at[yq], y_rs.at[yq], (yq * NZ + z, col))
        agg = agg + yrecv[yq].astype(F32)

    agg_b = agg.T.astype(BF16)
    term = lax.dot_general(feat[...], agg_b, (((0,), (0,)), ((), ())), preferred_element_type=F32)
    for q in range(NG):
        for t in range(8):
            r0 = q * 32 + (t // 2) * 8
            w1[q, t] = term[r0:r0 + 8, (t % 2) * 128:(t % 2 + 1) * 128]

    def step(src_of, land, k, me, peer):
        for o in (1, 7, 2, 6, 3, 5, 4):
            q = (me + o) % 8
            start(src_of(q), land.at[me], g_ss.at[k, q], g_rs.at[k, me], peer(q))

    def take(land, k, me, peer):
        for o in (1, 7, 2, 6, 3, 5, 4):
            q = (me + o) % 8
            arrived(land.at[q], g_rs.at[k, q], peer(q))

    step(lambda q: w1.at[q], r1, 0, g, g_peer)
    gi[...] = lax.dot_general(
        agg_b, wgt[...], (((1,), (1,)), ((), ())), preferred_element_type=F32
    ).astype(BF16)
    r1[g] = w1[g]
    take(r1, 0, g, g_peer)
    s1[...] = jnp.sum(r1[...], axis=0)
    step(lambda q: s1.at[q], r2, 1, y, y_peer)
    r2[y] = s1[y]
    take(r2, 1, y, y_peer)
    s2[...] = jnp.sum(r2[...], axis=0)
    step(lambda q: s2, r3, 2, z, z_peer)
    r3[z] = s2[...]
    take(r3, 2, z, z_peer)
    f1[y] = jnp.sum(r3[...], axis=0)
    step(lambda q: f1.at[y], f1, 3, y, y_peer)
    take(f1, 3, y, y_peer)
    f2[g] = f1[...]
    step(lambda q: f1, f2, 4, g, g_peer)
    take(f2, 4, g, g_peer)
    for q in range(NG):
        for t in range(8):
            r0 = q * 32 + (t // 2) * 8
            gw[r0:r0 + 8, (t % 2) * 128:(t % 2 + 1) * 128] = f2[q, t]
    for copy in sent:
        copy.wait_send()


def body(grad_out, relu_mask, features, weight, tile_values, tile_lists, tile_count):
    lists = tile_lists[0, 0]
    place = (lists[1] - lax.axis_index("col") * BC) * BR + lists[0] - lax.axis_index("row") * BR
    live = jnp.arange(CAP, dtype=jnp.int32) < tile_count[0, 0]
    hit = (place[None, :] == jnp.arange(BR * BC, dtype=jnp.int32)[:, None]) & live[None, :]
    table = jnp.min(jnp.where(hit, lists[2][None, :], CAP), axis=1)
    vmem = pl.BlockSpec(memory_space=pltpu.VMEM)
    dma = pltpu.SemaphoreType.DMA
    gi, gw = pl.pallas_call(
        kernel,
        out_shape=(jax.ShapeDtypeStruct((BLOCK, D), BF16), jax.ShapeDtypeStruct((D, D), F32)),
        in_specs=[vmem, vmem, vmem, vmem, pl.BlockSpec(memory_space=pl.ANY),
                  pl.BlockSpec(memory_space=pltpu.SMEM)],
        out_specs=(vmem, vmem),
        scratch_shapes=[
            pltpu.VMEM((CAP + 1, BLOCK, BLOCK), BF16),
            pltpu.VMEM((BR, D, BLOCK), BF16),
            pltpu.VMEM((D, BR * BLOCK), BF16),
            pltpu.VMEM((BR * BLOCK, 2 * BLOCK), BF16),
            pltpu.VMEM((NZ, NYL, D, BLOCK), F32),
            pltpu.VMEM((2, 4, NYL, D, BLOCK), BF16),
            pltpu.VMEM((2, 4, NYL, D, BLOCK), BF16),
            pltpu.VMEM((D, BLOCK), F32),
            pltpu.VMEM((NYL, D, BLOCK), BF16),
            pltpu.VMEM((NYL, D, BLOCK), BF16),
            pltpu.VMEM((NG, 8, 8, 128), F32),
            pltpu.VMEM((NG, 8, 8, 128), F32),
            pltpu.VMEM((8, 8, 128), F32),
            pltpu.VMEM((NY, 8, 128), F32),
            pltpu.VMEM((8, 128), F32),
            pltpu.VMEM((NZ, 8, 128), F32),
            pltpu.VMEM((NY, 8, 128), F32),
            pltpu.VMEM((NG, 8, 8, 128), F32),
            dma((4,)),
            dma((15, PIECES)), dma((16, PIECES)),
            dma((2, 4, NYL)), dma((2, 4, NYL)),
            dma((NYL,)), dma((NYL,)),
            dma((5, 8)), dma((5, 8)),
        ],
        compiler_params=pltpu.CompilerParams(
            collective_id=0, has_side_effects=True, vmem_limit_bytes=48 * 1024 * 1024
        ),
    )(grad_out, relu_mask, features[0], weight, tile_values[0, 0], table)
    return gi[None], gw


def solution(mesh):
    return jax.shard_map(
        body,
        mesh=mesh,
        in_specs=(
            P(("row", "col"), None),
            P(("row", "col"), None),
            P("col", "row", None),
            P(),
            P("row", "col", None, None, None),
            P("row", "col", None, None),
            P("row", "col"),
        ),
        out_specs=(P("col", "row", None), P()),
        check_vma=False,
    )
```

time: 603 us -> 90.9 us (0.15)
  waiting for transfers between devices: 493 us -> 0 us
  Pallas kernels: 0 us -> 81.3 us
  other arithmetic: 43.1 us -> 0.88 us
  local copies, waits for them, and re-layouts: 36.4 us -> 7.15 us
  matrix products: 15.4 us -> 0 us
  between operations: 14.5 us -> 1.31 us
    psum x1 -> x0, waiting for transfers between devices: 286 us -> none  [body(): grad_weight = lax.psum(weight_term, ('row', 'col'))]
    reduce_scatter x1 -> x0, waiting for transfers between devices: 145 us -> none  [body(): lax.psum_scatter(partial_sum, 'row', scatter_dimension=0, tiled=True)]
    pallas_call x0 -> x1, Pallas kernels: none -> 81.3 us  [body(): pl.pallas_call(kernel, out_shape=(jax.ShapeDtypeStruct((BLOCK, D), BF16),...]
    all_gather x1 -> x0, waiting for transfers between devices: 61.9 us -> none  [body(): gathered = lax.all_gather(dz, 'col', axis=0, tiled=True)]
    scatter-add x1 -> x0, other arithmetic: 40.8 us -> none  [body(): jnp.zeros((cols_blocks, block, width), jnp.float32).at[targets]]
    dot_general x1 -> x0, local copies, waits for them, and re-layouts: 18.6 us -> none  [body(): jnp.einsum('tik,tid->tkd', tile_values[0, 0], blocks, preferred_element_t...]
    dot_general x3 -> x0, matrix products: 15.4 us -> none  [the longest x1 11.9 us: body(): jnp.einsum('tik,tid->tkd', tile_values[0, 0], blocks, preferred_element_t...]
    gather x3 -> x0, local copies, waits for them, and re-layouts: 11.7 us -> none  [the longest x1 8.45 us: body(): blocks = gathered.reshape(rows_blocks, block, width)[block_rows]]
  transfers between devices with their start and end apart: 3 -> 0, of which waited for: 3 -> 0; matrix products, arithmetic and copies ran while one was open for 1% -> 0% of each run, Pallas kernels for 0% -> 0%
where the time goes in v1:
time: 90.9 us; the launch traced here: 90.6 us
  Pallas kernels  81.3 us (89%)
  local copies, waits for them, and re-layouts  7.15 us (8%)
  between operations  1.31 us (1%)
    pallas_call x1, Pallas kernels, body(): pl.pallas_call(kernel, out_shape=(jax.ShapeDtypeStruct((BLOCK, D), BF16),...  81.3 us
    unnamed x12, local copies, waits for them, and re-layouts  7.15 us

profile of v1, /device:TPU:1, one launch (start us, length us, event | category | flops | bytes accessed | tf_op | source)
XLA Modules:
  0.0 90.6 jit_solution(4397662356132765133)
XLA Ops:
  1.3 0.7 add_subtract_fusion
  2.0 0.1 select_reduce_fusion.table
  2.2 0.0 copy-start
  2.2 2.3 %copy-done = bf16[1,1,144,128,128]{4,3,2,1,0:T(8,128)(2,1)S(1)} copy-done((bf16[1,1,144,128,128]{4,3,2,1,0:T(8,128)(2,1)S(1)}, bf16[1,1,144,128,128]{4,3,2,1,0:T(8,128)(2,1)}, u32[]{:S(2)}) %copy-start) | copy-done | bytes 4718616
  4.5 0.0 copy-start.1
  4.5 0.9 copy-done.1
  5.4 0.0 copy-start.2
  5.4 0.9 copy-done.2
  6.3 0.0 copy-start.3
  6.3 0.8 copy-done.3
  7.2 0.0 copy-start.4
  7.2 0.8 copy-done.4
  8.0 81.3 %shard_map.86 = (bf16[128,256]{1,0:T(8,128)(2,1)S(1)}, f32[256,256]{1,0:T(8,128)S(1)}) custom-call(bf16[128,256]{1,0:T(8,128)(2,1)S(1)} %copy-done.3, s32[128,256]{1,0:T(8,128)S(1)} %copy-done.1, bf16[128,256]{1,0:T(8,128)(2,1)S(1)} %bitcast.8, bf16[256,256]{1,0:T(8,128)(2,1)S(1)} %copy-done.2, bf16[144,128,128]{2,1,0:T(8,128)(2,1)S(1)} %bitcast.7, ...), custom_call_target="tpu_custom_call" | custom-call | tf_op jit(solution)/shard_map/pallas_call | solution.py:224
  89.3 0.6 copy.12
  89.9 0.7 copy.13
  (1 shorter events, 0.0 us)
Async XLA Ops:
  2.2 2.3 %copy-start = (bf16[1,1,144,128,128]{4,3,2,1,0:T(8,128)(2,1)S(1)}, bf16[1,1,144,128,128]{4,3,2,1,0:T(8,128)(2,1)}, u32[]{:S(2)}) copy-start(bf16[1,1,144,128,128]{4,3,2,1,0:T(8,128)(2,1)} %param.11) | copy-start | bytes 14155780
  4.5 0.9 copy-start.1
  5.4 0.9 copy-start.2
  6.3 0.8 copy-start.3
  7.2 0.8 copy-start.4

commit v2 on v1

v2 whole, which is shorter than its diff:
```python
import jax
import jax.numpy as jnp
from jax import lax
from jax.experimental import pallas as pl
from jax.experimental.pallas import tpu as pltpu
from jax.sharding import PartitionSpec as P

NZ, NYL, NX, NY, NG = 8, 4, 4, 8, 8
BLOCK, D = 128, 256
BR, BC, CAP = 16, 32, 144
HALF = D // 2
EARLY, BEFORE = 6, 16
F32, BF16 = jnp.float32, jnp.bfloat16


def kernel(
    go_hbm, mask_hbm, feat_hbm, wgt_hbm, tiles, lists_hbm, count_hbm, gi, gw,
    go, mask, feat, wgt, lists, count, table_v, table, tiles_v,
    ag, dzall, part, zsend, zrecv, own, ysend, yrecv, feats, inner,
    w1, r1, s1, r2, s2, r3, f1, f1b, f2,
    in_sem, tile_sem, ag_ss, ag_rs, fy_ss, f_ss, f_rs, z_ss, z_rs,
    y_ss, y_rs, g_ss, g_rs,
):
    row, col = lax.axis_index("row"), lax.axis_index("col")
    ylo, z = row // NZ, row % NZ
    x, yh, core = col // 4, (col // 2) % 2, col % 2
    g = x * 2 + core
    y = yh * NYL + ylo

    def g_peer(q):
        return row, (q // 2) * 4 + yh * 2 + q % 2

    def y_peer(q):
        return (q % NYL) * NZ + z, x * 4 + (q // NYL) * 2 + core

    def z_peer(q):
        return ylo * NZ + q, col

    def yl_peer(q):
        return q * NZ + z, col

    def remote(src, dst, ssem, rsem, to):
        return pltpu.make_async_remote_copy(
            src_ref=src, dst_ref=dst, send_sem=ssem, recv_sem=rsem,
            device_id=to, device_id_type=pl.DeviceIdType.MESH,
        )

    sent = []

    def start(src, dst, ssem, rsem, to):
        copy = remote(src, dst, ssem, rsem, to)
        copy.start()
        sent.append(copy)

    def arrived(dst, sem, frm):
        remote(dst, dst, sem, sem, frm).wait_recv()

    barrier = pltpu.get_barrier_semaphore()
    for o in (4, 3, 5, 2, 6, 1, 7):
        for to in (y_peer((y + o) % NY), z_peer((z + o) % NZ), g_peer((g + o) % NG)):
            pl.semaphore_signal(barrier, inc=1, device_id=to, device_id_type=pl.DeviceIdType.MESH)
    fetched = []
    for i, (src, dst) in enumerate((
        (go_hbm, go), (mask_hbm, mask), (feat_hbm.at[0], feat), (wgt_hbm, wgt),
        (lists_hbm.at[0], lists), (count_hbm, count),
    )):
        copy = pltpu.make_async_copy(src, dst, in_sem.at[i])
        copy.start()
        fetched.append(copy)
    tile_copies = []
    for i in range(4):
        part_of = pl.ds(i * (CAP // 4), CAP // 4)
        copy = pltpu.make_async_copy(tiles.at[0, 0, part_of], tiles_v.at[part_of], tile_sem.at[i])
        copy.start()
        tile_copies.append(copy)
    fetched[0].wait()
    fetched[1].wait()
    dz = go[...].astype(F32) * mask[...].astype(F32)
    ag[col] = dz.T.astype(BF16)
    fetched[2].wait()
    feats[2, ylo] = feat[...].astype(F32).T.astype(BF16)
    pl.semaphore_wait(barrier, 21)

    def slot_of(xq, yq, cq):
        return xq * 4 + yq * 2 + cq

    def ag_send(slot, to_col, k):
        start(ag.at[slot], ag.at[slot], ag_ss.at[k], ag_rs.at[slot], (row, to_col))

    def ag_wait(slot, from_col):
        arrived(ag.at[slot], ag_rs.at[slot], (row, from_col))

    xs = [(x + o) % NX for o in (2, 1, 3)]
    over = slot_of(x, 1 - yh, core)
    ag_send(col, over, 0)
    for k, xq in enumerate(xs):
        ag_send(col, slot_of(xq, yh, core), 1 + k)
    ag_send(col, slot_of(x, yh, 1 - core), 4)
    fetched[4].wait()
    fetched[5].wait()
    tiles_v[CAP] = jnp.zeros((BLOCK, BLOCK), BF16)
    place = (lists[1] - col * BC) * BR + lists[0] - row * BR
    live = lax.broadcasted_iota(jnp.int32, (1, CAP), 1) < count[0, 0]
    place = jnp.broadcast_to(jnp.where(live, place, -1), (BLOCK, CAP)).T
    slots = jnp.broadcast_to(lists[2], (BLOCK, CAP)).T
    lane = lax.broadcasted_iota(jnp.int32, (CAP, BLOCK), 1)
    for b in range(NYL):
        table_v[b:b + 1] = jnp.min(
            jnp.where(place == lane + b * BLOCK, slots, CAP), axis=0, keepdims=True
        )
    table_copy = pltpu.make_async_copy(table_v, table, in_sem.at[6])
    table_copy.start()

    for o in (2, 1, 3):
        q = (ylo + o) % NYL
        start(feats.at[2, ylo], feats.at[2, ylo], fy_ss.at[q], f_rs.at[2, ylo], yl_peer(q))
    up, down = z_peer((z + 1) % NZ), z_peer((z + NZ - 1) % NZ)

    def feat_along(yq, src_up, src_down):
        for src, dst, to in ((src_up, src_up - 1, up), (src_down, src_down + 1, down)):
            start(feats.at[src, yq], feats.at[dst, yq], f_ss.at[dst, yq], f_rs.at[dst, yq], to)

    def feat_wait(at, yq, frm):
        arrived(feats.at[at, yq], f_rs.at[at, yq], frm)

    ag_wait(over, over)
    for k, xq in enumerate(xs):
        ag_send(over, slot_of(xq, yh, core), 5 + k)
    ag_send(over, slot_of(x, yh, 1 - core), 8)
    for k, xq in enumerate(xs):
        ag_wait(slot_of(xq, yh, core), slot_of(xq, yh, core))
        ag_send(slot_of(xq, yh, core), slot_of(x, yh, 1 - core), 9 + k)

    sides = (yh, 1 - yh)

    def fill(side):
        for k in range(8):
            at = (side * 8 + k) * BLOCK
            dzall[:, at:at + BLOCK] = ag[slot_of(k // 2, sides[side], k % 2)]

    def product(zq, h, side):
        first = zq * BR + sides[side] * 2
        rhs = jnp.concatenate([
            jnp.concatenate(
                [tiles_v[table[2 * h + j, first + (k // 2) * 4 + k % 2]] for k in range(8)], axis=0
            )
            for j in range(2)
        ], axis=1)
        lhs = dzall[:, side * 8 * BLOCK:(side + 1) * 8 * BLOCK]
        return jnp.dot(lhs, rhs, preferred_element_type=F32)

    def first_half(t, carry):
        zq, h = t // 2, t % 2
        res = product(zq, h, 0)
        part[zq, 2 * h] = res[:, :BLOCK]
        part[zq, 2 * h + 1] = res[:, BLOCK:]
        return carry

    for xq in range(NX):
        ag_wait(slot_of(xq, yh, 1 - core), slot_of(x, yh, 1 - core))
    table_copy.wait()
    for copy in tile_copies + fetched[3:4]:
        copy.wait()
    fill(0)
    lax.fori_loop(0, EARLY, first_half, 0)
    for o in (0, 1, 3, 2):
        q = (ylo + o) % NYL
        if o:
            feat_wait(2, q, yl_peer(q))
        feat_along(q, 2, 2)
    lax.fori_loop(EARLY, BEFORE, first_half, 0)
    for k, xq in enumerate(xs):
        ag_wait(slot_of(xq, 1 - yh, core), slot_of(xq, yh, core))
        ag_send(slot_of(xq, 1 - yh, core), slot_of(x, yh, 1 - core), 12 + k)
    if BEFORE < 2 * NZ:
        lax.fori_loop(BEFORE, 2 * NZ, first_half, 0)
    for xq in range(NX):
        ag_wait(slot_of(xq, 1 - yh, 1 - core), slot_of(x, yh, 1 - core))
    fill(1)

    def compute(zq):
        def second_half(h, carry):
            res = product(zq, h, 1)
            part[zq, 2 * h] += res[:, :BLOCK]
            part[zq, 2 * h + 1] += res[:, BLOCK:]
            return carry

        lax.fori_loop(0, NYL // 2, second_half, 0)
    ways = (up, down)
    order = [(ylo + o) % NYL for o in (2, 1, 3, 0)]

    def chain(s):
        for yq in order:
            for d in range(2):
                dest = (z + 4 - s) % NZ if d == 0 else (z + 4 + s) % NZ
                mine = pl.ds(d * HALF, HALF)
                if s == 0:
                    zsend[d, s, yq, mine] = part[dest, yq, mine].astype(BF16)
                    src, dst = zsend.at[d, s, yq, mine], zrecv.at[d, s, yq, mine]
                elif s == 1:
                    arrived(zrecv.at[d, 0, yq, mine], z_rs.at[d, 0, yq], ways[1 - d])
                    other = pl.ds((1 - d) * HALF, HALF)
                    got = part[dest, yq, mine] + zrecv[d, 0, yq, mine].astype(F32)
                    zsend[d, s, yq, mine] = got.astype(BF16)
                    zsend[d, s, yq, other] = part[dest, yq, other].astype(BF16)
                    src, dst = zsend.at[d, s, yq], zrecv.at[d, s, yq]
                else:
                    arrived(zrecv.at[d, s - 1, yq], z_rs.at[d, s - 1, yq], ways[1 - d])
                    got = part[dest, yq] + zrecv[d, s - 1, yq].astype(F32)
                    zsend[d, s, yq] = got.astype(BF16)
                    src, dst = zsend.at[d, s, yq], zrecv.at[d, s, yq]
                start(src, dst, z_ss.at[d, s, yq], z_rs.at[d, s, yq], ways[d])

    def weight_term(lefts, rights):
        return lax.dot_general(
            jnp.concatenate(lefts, axis=1), jnp.concatenate(rights, axis=1),
            (((1,), (1,)), ((), ())), preferred_element_type=F32,
        )

    compute((z + 4) % NZ)
    chain(0)
    for yq in order[::-1]:
        feat_wait(1, yq, down)
        feat_wait(3, yq, up)
        feat_along(yq, 1, 3)
    compute((z + 3) % NZ)
    compute((z + 5) % NZ)
    chain(1)
    for o in (2, 6, 1, 7, 0):
        compute((z + o) % NZ)
    inner[...] = weight_term(
        [feats[2 + i, q] for i in (-1, 0, 1) for q in range(NYL)],
        [part[(z + NZ + i) % NZ, q].astype(BF16) for i in (-1, 0, 1) for q in range(NYL)],
    )
    chain(2)
    for yq in order[::-1]:
        feat_wait(0, yq, down)
        feat_wait(4, yq, up)
    term = (inner[...] + weight_term(
        [feats[i, q] for i in (4, 0) for q in range(NYL)],
        [zsend[d, 2, q] for d in range(2) for q in range(NYL)],
    )).astype(BF16)
    for q in range(NG):
        w1[q, :32] = term[q * 32:(q + 1) * 32, :128]
        w1[q, 32:] = term[q * 32:(q + 1) * 32, 128:]

    def step(src_of, land, k, me, peer):
        for o in (4, 3, 5, 2, 6, 1, 7):
            q = (me + o) % 8
            start(src_of(q), land.at[me], g_ss.at[k, q], g_rs.at[k, me], peer(q))

    def take(land, k, me, peer):
        for o in (1, 7, 2, 6, 3, 5, 4):
            q = (me + o) % 8
            arrived(land.at[q], g_rs.at[k, q], peer(q))

    step(lambda q: w1.at[q], r1, 0, g, g_peer)
    r1[g] = w1[g]
    take(r1, 0, g, g_peer)
    s1[...] = jnp.sum(r1[...].astype(F32), axis=0)
    step(lambda q: s1.at[pl.ds(pl.multiple_of(q * 8, 8), 8)], r2, 1, y, y_peer)
    r2[y] = s1[pl.ds(pl.multiple_of(y * 8, 8), 8)]
    chain(3)
    take(r2, 1, y, y_peer)
    s2[...] = jnp.sum(r2[...], axis=0)
    step(lambda q: s2, r3, 2, z, z_peer)
    r3[z] = s2[...]
    take(r3, 2, z, z_peer)
    f1[y] = jnp.sum(r3[...], axis=0)
    step(lambda q: f1.at[y], f1, 3, y, y_peer)
    for k, yq in enumerate(order):
        for d in range(2):
            arrived(zrecv.at[d, 3, yq], z_rs.at[d, 3, yq], ways[1 - d])
        total = part[z, yq] + zrecv[0, 3, yq].astype(F32) + zrecv[1, 3, yq].astype(F32)
        if k < 3:
            ysend[yq] = total.astype(BF16)
            start(ysend.at[yq], yrecv.at[ylo], y_ss.at[yq], y_rs.at[ylo], yl_peer(yq))
        else:
            own[...] = total
    take(f1, 3, y, y_peer)
    f1b[...] = f1[...].reshape(64, 128).astype(BF16)
    f2[g] = f1b[...]
    step(lambda q: f1b, f2, 4, g, g_peer)

    agg = own[...]
    for yq in order[:3]:
        arrived(yrecv.at[yq], y_rs.at[yq], yl_peer(yq))
        agg = agg + yrecv[yq].astype(F32)
    gi[...] = lax.dot_general(
        agg.T.astype(BF16), wgt[...], (((1,), (1,)), ((), ())), preferred_element_type=F32
    ).astype(BF16)
    take(f2, 4, g, g_peer)
    for q in range(NG):
        gw[q * 32:(q + 1) * 32, :128] = f2[q, :32].astype(F32)
        gw[q * 32:(q + 1) * 32, 128:] = f2[q, 32:].astype(F32)
    for copy in sent:
        copy.wait_send()


def body(grad_out, relu_mask, features, weight, tile_values, tile_lists, tile_count):
    vmem = pl.BlockSpec(memory_space=pltpu.VMEM)
    dma = pltpu.SemaphoreType.DMA
    gi, gw = pl.pallas_call(
        kernel,
        out_shape=(jax.ShapeDtypeStruct((BLOCK, D), BF16), jax.ShapeDtypeStruct((D, D), F32)),
        in_specs=[pl.BlockSpec(memory_space=pl.ANY)] * 7,
        out_specs=(vmem, vmem),
        scratch_shapes=[
            pltpu.VMEM((BLOCK, D), BF16),
            pltpu.VMEM((BLOCK, D), jnp.int32),
            pltpu.VMEM((BLOCK, D), BF16),
            pltpu.VMEM((D, D), BF16),
            pltpu.VMEM((3, 1, CAP), jnp.int32),
            pltpu.SMEM((1, 1), jnp.int32),
            pltpu.VMEM((NYL, BLOCK), jnp.int32),
            pltpu.SMEM((NYL, BLOCK), jnp.int32),
            pltpu.VMEM((CAP + 1, BLOCK, BLOCK), BF16),
            pltpu.VMEM((BR, D, BLOCK), BF16),
            pltpu.VMEM((D, BR * BLOCK), BF16),
            pltpu.VMEM((NZ, NYL, D, BLOCK), F32),
            pltpu.VMEM((2, 4, NYL, D, BLOCK), BF16),
            pltpu.VMEM((2, 4, NYL, D, BLOCK), BF16),
            pltpu.VMEM((D, BLOCK), F32),
            pltpu.VMEM((NYL, D, BLOCK), BF16),
            pltpu.VMEM((NYL, D, BLOCK), BF16),
            pltpu.VMEM((5, NYL, D, BLOCK), BF16),
            pltpu.VMEM((D, D), F32),
            pltpu.VMEM((NG, 64, 128), BF16),
            pltpu.VMEM((NG, 64, 128), BF16),
            pltpu.VMEM((64, 128), F32),
            pltpu.VMEM((NY, 8, 128), F32),
            pltpu.VMEM((8, 128), F32),
            pltpu.VMEM((NZ, 8, 128), F32),
            pltpu.VMEM((NY, 8, 128), F32),
            pltpu.VMEM((64, 128), BF16),
            pltpu.VMEM((NG, 64, 128), BF16),
            dma((7,)), dma((4,)),
            dma((15,)), dma((16,)),
            dma((NYL,)), dma((5, NYL)), dma((5, NYL)),
            dma((2, 4, NYL)), dma((2, 4, NYL)),
            dma((NYL,)), dma((NYL,)),
            dma((5, 8)), dma((5, 8)),
        ],
        compiler_params=pltpu.CompilerParams(
            collective_id=0, has_side_effects=True, vmem_limit_bytes=48 * 1024 * 1024
        ),
    )(
        *(pltpu.with_memory_space_constraint(a, pltpu.HBM) for a in (
            grad_out, relu_mask, features, weight, tile_values, tile_lists.transpose(0, 2, 1, 3)
        )),
        tile_count,
    )
    return gi[None], gw


def solution(mesh):
    return jax.shard_map(
        body,
        mesh=mesh,
        in_specs=(
            P(("row", "col"), None),
            P(("row", "col"), None),
            P("col", "row", None),
            P(),
            P("row", "col", None, None, None),
            P("row", "col", None, None),
            P("row", "col"),
        ),
        out_specs=(P("col", "row", None), P()),
        check_vma=False,
    )
```

time: 90.9 us -> 75.6 us (0.83)
  Pallas kernels: 81.3 us -> 72.8 us
  local copies, waits for them, and re-layouts: 7.15 us -> 1.33 us
    pallas_call x1, Pallas kernels: 81.3 us -> 72.8 us  [body(): pl.pallas_call(kernel, out_shape=(jax.ShapeDtypeStruct((BLOCK, D), BF16),...]
    unnamed x12 -> x2, local copies, waits for them, and re-layouts: 7.15 us -> 1.33 us
where the time goes in v2:
time: 75.6 us; the launch traced here: 75.4 us
  Pallas kernels  72.8 us (96%)
  local copies, waits for them, and re-layouts  1.33 us (2%)
  between operations  1.29 us (2%)
    pallas_call x1, Pallas kernels, body(): pl.pallas_call(kernel, out_shape=(jax.ShapeDtypeStruct((BLOCK, D), BF16),...  72.8 us

profile of v2, /device:TPU:1, one launch (start us, length us, event | category | flops | bytes accessed | tf_op | source)
XLA Modules:
  0.0 75.4 jit_solution(5547421737250759165)
XLA Ops:
  1.3 72.8 %shard_map.86 = (bf16[128,256]{1,0:T(8,128)(2,1)S(1)}, f32[256,256]{1,0:T(8,128)S(1)}) custom-call(bf16[128,256]{1,0:T(8,128)(2,1)} %go_hbm.1, s32[128,256]{1,0:T(8,128)} %mask_hbm.1, bf16[1,128,256]{2,1,0:T(8,128)(2,1)} %feat_hbm.1, bf16[256,256]{1,0:T(8,128)(2,1)} %wgt_hbm.1, bf16[1,1,144,128,128]{4,3,2,1,0:T(8,128)(2,1)} %tiles.1, ...), custom_call_target="tpu_custom_call" | custom-call | tf_op jit(solution)/shard_map/pallas_call | solution.py:303
  74.1 0.6 copy.12
  74.7 0.7 copy.13

commit v3 on v2

--- a/solution.py
+++ b/solution.py
@@ -9,7 +9,7 @@
 BLOCK, D = 128, 256
 BR, BC, CAP = 16, 32, 144
 HALF = D // 2
-EARLY, BEFORE = 6, 16
+EARLY, BEFORE = 2, 8
 F32, BF16 = jnp.float32, jnp.bfloat16
 
 
@@ -79,23 +79,6 @@
     ag[col] = dz.T.astype(BF16)
     fetched[2].wait()
     feats[2, ylo] = feat[...].astype(F32).T.astype(BF16)
-    pl.semaphore_wait(barrier, 21)
-
-    def slot_of(xq, yq, cq):
-        return xq * 4 + yq * 2 + cq
-
-    def ag_send(slot, to_col, k):
-        start(ag.at[slot], ag.at[slot], ag_ss.at[k], ag_rs.at[slot], (row, to_col))
-
-    def ag_wait(slot, from_col):
-        arrived(ag.at[slot], ag_rs.at[slot], (row, from_col))
-
-    xs = [(x + o) % NX for o in (2, 1, 3)]
-    over = slot_of(x, 1 - yh, core)
-    ag_send(col, over, 0)
-    for k, xq in enumerate(xs):
-        ag_send(col, slot_of(xq, yh, core), 1 + k)
-    ag_send(col, slot_of(x, yh, 1 - core), 4)
     fetched[4].wait()
     fetched[5].wait()
     tiles_v[CAP] = jnp.zeros((BLOCK, BLOCK), BF16)
@@ -110,15 +93,38 @@
         )
     table_copy = pltpu.make_async_copy(table_v, table, in_sem.at[6])
     table_copy.start()
-
-    for o in (2, 1, 3):
-        q = (ylo + o) % NYL
-        start(feats.at[2, ylo], feats.at[2, ylo], fy_ss.at[q], f_rs.at[2, ylo], yl_peer(q))
+    pl.semaphore_wait(barrier, 21)
+
+    def slot_of(xq, yq, cq):
+        return xq * 4 + yq * 2 + cq
+
+    def ag_send(slot, to_col, k):
+        start(ag.at[slot], ag.at[slot], ag_ss.at[k], ag_rs.at[slot], (row, to_col))
+
+    def ag_wait(slot, from_col):
+        arrived(ag.at[slot], ag_rs.at[slot], (row, from_col))
+
+    xs = [(x + o) % NX for o in (2, 1, 3)]
+    over = slot_of(x, 1 - yh, core)
+    ag_send(col, over, 0)
+    for k, xq in enumerate(xs):
+        ag_send(col, slot_of(xq, yh, core), 1 + k)
+    ag_send(col, slot_of(x, yh, 1 - core), 4)
     up, down = z_peer((z + 1) % NZ), z_peer((z + NZ - 1) % NZ)
-
-    def feat_along(yq, src_up, src_down):
-        for src, dst, to in ((src_up, src_up - 1, up), (src_down, src_down + 1, down)):
-            start(feats.at[src, yq], feats.at[dst, yq], f_ss.at[dst, yq], f_rs.at[dst, yq], to)
+    up2, down2 = z_peer((z + 2) % NZ), z_peer((z + NZ - 2) % NZ)
+    for dst, to in ((0, up2), (4, down2)):
+        start(feats.at[2, ylo], feats.at[dst, ylo], f_ss.at[dst, ylo], f_rs.at[dst, ylo], to)
+
+    def feat_over_y(at):
+        for o in (2, 1, 3):
+            q = (ylo + o) % NYL
+            start(feats.at[at, ylo], feats.at[at, ylo], fy_ss.at[at, q], f_rs.at[at, ylo], yl_peer(q))
+
+    feat_over_y(2)
+
+    def feat_along(yq):
+        for dst, to in ((1, up), (3, down)):
+            start(feats.at[2, yq], feats.at[dst, yq], f_ss.at[dst, yq], f_rs.at[dst, yq], to)
 
     def feat_wait(at, yq, frm):
         arrived(feats.at[at, yq], f_rs.at[at, yq], frm)
@@ -130,6 +136,8 @@
     for k, xq in enumerate(xs):
         ag_wait(slot_of(xq, yh, core), slot_of(xq, yh, core))
         ag_send(slot_of(xq, yh, core), slot_of(x, yh, 1 - core), 9 + k)
+
+    feat_along(ylo)
 
     sides = (yh, 1 - yh)
 
@@ -163,15 +171,18 @@
         copy.wait()
     fill(0)
     lax.fori_loop(0, EARLY, first_half, 0)
-    for o in (0, 1, 3, 2):
-        q = (ylo + o) % NYL
-        if o:
-            feat_wait(2, q, yl_peer(q))
-        feat_along(q, 2, 2)
     lax.fori_loop(EARLY, BEFORE, first_half, 0)
     for k, xq in enumerate(xs):
         ag_wait(slot_of(xq, 1 - yh, core), slot_of(xq, yh, core))
         ag_send(slot_of(xq, 1 - yh, core), slot_of(x, yh, 1 - core), 12 + k)
+    for o in (1, 3, 2):
+        q = (ylo + o) % NYL
+        feat_wait(2, q, yl_peer(q))
+        feat_along(q)
+    feat_wait(0, ylo, down2)
+    feat_wait(4, ylo, up2)
+    feat_over_y(0)
+    feat_over_y(4)
     if BEFORE < 2 * NZ:
         lax.fori_loop(BEFORE, 2 * NZ, first_half, 0)
     for xq in range(NX):
@@ -219,23 +230,22 @@
 
     compute((z + 4) % NZ)
     chain(0)
-    for yq in order[::-1]:
-        feat_wait(1, yq, down)
-        feat_wait(3, yq, up)
-        feat_along(yq, 1, 3)
     compute((z + 3) % NZ)
     compute((z + 5) % NZ)
     chain(1)
     for o in (2, 6, 1, 7, 0):
         compute((z + o) % NZ)
+    for yq in order[::-1]:
+        feat_wait(1, yq, down)
+        feat_wait(3, yq, up)
     inner[...] = weight_term(
         [feats[2 + i, q] for i in (-1, 0, 1) for q in range(NYL)],
         [part[(z + NZ + i) % NZ, q].astype(BF16) for i in (-1, 0, 1) for q in range(NYL)],
     )
     chain(2)
-    for yq in order[::-1]:
-        feat_wait(0, yq, down)
-        feat_wait(4, yq, up)
+    for yq in order[:3]:
+        feat_wait(0, yq, yl_peer(yq))
+        feat_wait(4, yq, yl_peer(yq))
     term = (inner[...] + weight_term(
         [feats[i, q] for i in (4, 0) for q in range(NYL)],
         [zsend[d, 2, q] for d in range(2) for q in range(NYL)],
@@ -336,7 +346,7 @@
             pltpu.VMEM((NG, 64, 128), BF16),
             dma((7,)), dma((4,)),
             dma((15,)), dma((16,)),
-            dma((NYL,)), dma((5, NYL)), dma((5, NYL)),
+            dma((5, NYL)), dma((5, NYL)), dma((5, NYL)),
             dma((2, 4, NYL)), dma((2, 4, NYL)),
             dma((NYL,)), dma((NYL,)),
             dma((5, 8)), dma((5, 8)),

time: 75.6 us -> 69.7 us (0.922)
  Pallas kernels: 72.8 us -> 67 us
    pallas_call x1, Pallas kernels: 72.8 us -> 67 us  [body(): pl.pallas_call(kernel, out_shape=(jax.ShapeDtypeStruct((BLOCK, D), BF16),...]
where the time goes in v3:
time: 69.7 us; the launch traced here: 69.6 us
  Pallas kernels  67 us (96%)
  local copies, waits for them, and re-layouts  1.33 us (2%)
  between operations  1.29 us (2%)
    pallas_call x1, Pallas kernels, body(): pl.pallas_call(kernel, out_shape=(jax.ShapeDtypeStruct((BLOCK, D), BF16),...  67 us

profile of v3, /device:TPU:1, one launch (start us, length us, event | category | flops | bytes accessed | tf_op | source)
XLA Modules:
  0.0 69.6 jit_solution(683858933937587620)
XLA Ops:
  1.3 67.0 %shard_map.86 = (bf16[128,256]{1,0:T(8,128)(2,1)S(1)}, f32[256,256]{1,0:T(8,128)S(1)}) custom-call(bf16[128,256]{1,0:T(8,128)(2,1)} %go_hbm.1, s32[128,256]{1,0:T(8,128)} %mask_hbm.1, bf16[1,128,256]{2,1,0:T(8,128)(2,1)} %feat_hbm.1, bf16[256,256]{1,0:T(8,128)(2,1)} %wgt_hbm.1, bf16[1,1,144,128,128]{4,3,2,1,0:T(8,128)(2,1)} %tiles.1, ...), custom_call_target="tpu_custom_call" | custom-call | tf_op jit(solution)/shard_map/pallas_call | solution.py:313
  68.3 0.6 copy.12
  68.9 0.7 %copy.13 = f32[256,256]{1,0:T(8,128)} copy(f32[256,256]{1,0:T(8,128)S(1)} %get-tuple-element.9) | data formatting | bytes 524288

commit v4 on v3

--- a/solution.py
+++ b/solution.py
@@ -275,9 +275,6 @@
     s2[...] = jnp.sum(r2[...], axis=0)
     step(lambda q: s2, r3, 2, z, z_peer)
     r3[z] = s2[...]
-    take(r3, 2, z, z_peer)
-    f1[y] = jnp.sum(r3[...], axis=0)
-    step(lambda q: f1.at[y], f1, 3, y, y_peer)
     for k, yq in enumerate(order):
         for d in range(2):
             arrived(zrecv.at[d, 3, yq], z_rs.at[d, 3, yq], ways[1 - d])
@@ -287,6 +284,9 @@
             start(ysend.at[yq], yrecv.at[ylo], y_ss.at[yq], y_rs.at[ylo], yl_peer(yq))
         else:
             own[...] = total
+    take(r3, 2, z, z_peer)
+    f1[y] = jnp.sum(r3[...], axis=0)
+    step(lambda q: f1.at[y], f1, 3, y, y_peer)
     take(f1, 3, y, y_peer)
     f1b[...] = f1[...].reshape(64, 128).astype(BF16)
     f2[g] = f1b[...]

time: 69.7 us -> 69 us (0.990)
  Pallas kernels: 67 us -> 66.3 us
    pallas_call x1, Pallas kernels: 67 us -> 66.3 us  [body(): pl.pallas_call(kernel, out_shape=(jax.ShapeDtypeStruct((BLOCK, D), BF16),...]
where the time goes in v4:
time: 69 us; the launch traced here: 68.9 us
  Pallas kernels  66.3 us (96%)
  local copies, waits for them, and re-layouts  1.33 us (2%)
  between operations  1.29 us (2%)
    pallas_call x1, Pallas kernels, body(): pl.pallas_call(kernel, out_shape=(jax.ShapeDtypeStruct((BLOCK, D), BF16),...  66.3 us

profile of v4, /device:TPU:1, one launch (start us, length us, event | category | flops | bytes accessed | tf_op | source)
XLA Modules:
  0.0 68.9 jit_solution(14662475936745191969)
XLA Ops:
  1.3 66.3 %shard_map.86 = (bf16[128,256]{1,0:T(8,128)(2,1)S(1)}, f32[256,256]{1,0:T(8,128)S(1)}) custom-call(bf16[128,256]{1,0:T(8,128)(2,1)} %go_hbm.1, s32[128,256]{1,0:T(8,128)} %mask_hbm.1, bf16[1,128,256]{2,1,0:T(8,128)(2,1)} %feat_hbm.1, bf16[256,256]{1,0:T(8,128)(2,1)} %wgt_hbm.1, bf16[1,1,144,128,128]{4,3,2,1,0:T(8,128)(2,1)} %tiles.1, ...), custom_call_target="tpu_custom_call" | custom-call | tf_op jit(solution)/shard_map/pallas_call | solution.py:313
  67.6 0.6 copy.12
  68.2 0.7 %copy.13 = f32[256,256]{1,0:T(8,128)} copy(f32[256,256]{1,0:T(8,128)S(1)} %get-tuple-element.9) | data formatting | bytes 524288

commit v5 on v4

--- a/solution.py
+++ b/solution.py
@@ -232,8 +232,10 @@
     chain(0)
     compute((z + 3) % NZ)
     compute((z + 5) % NZ)
+    compute((z + 2) % NZ)
+    compute((z + 6) % NZ)
     chain(1)
-    for o in (2, 6, 1, 7, 0):
+    for o in (1, 7, 0):
         compute((z + o) % NZ)
     for yq in order[::-1]:
         feat_wait(1, yq, down)

time: 69 us -> 69.6 us (level)
  no operation moved by 1% of the time
where the time goes in v5:
time: 69.6 us; the launch traced here: 69.5 us
  Pallas kernels  66.8 us (96%)
  local copies, waits for them, and re-layouts  1.33 us (2%)
  between operations  1.29 us (2%)
    pallas_call x1, Pallas kernels, body(): pl.pallas_call(kernel, out_shape=(jax.ShapeDtypeStruct((BLOCK, D), BF16),...  66.8 us

profile of v5, /device:TPU:1, one launch (start us, length us, event | category | flops | bytes accessed | tf_op | source)
XLA Modules:
  0.0 69.5 jit_solution(15837837874918810624)
XLA Ops:
  1.3 66.8 %shard_map.86 = (bf16[128,256]{1,0:T(8,128)(2,1)S(1)}, f32[256,256]{1,0:T(8,128)S(1)}) custom-call(bf16[128,256]{1,0:T(8,128)(2,1)} %go_hbm.1, s32[128,256]{1,0:T(8,128)} %mask_hbm.1, bf16[1,128,256]{2,1,0:T(8,128)(2,1)} %feat_hbm.1, bf16[256,256]{1,0:T(8,128)(2,1)} %wgt_hbm.1, bf16[1,1,144,128,128]{4,3,2,1,0:T(8,128)(2,1)} %tiles.1, ...), custom_call_target="tpu_custom_call" | custom-call | tf_op jit(solution)/shard_map/pallas_call | solution.py:315
  68.1 0.6 copy.12
  68.8 0.7 %copy.13 = f32[256,256]{1,0:T(8,128)} copy(f32[256,256]{1,0:T(8,128)S(1)} %get-tuple-element.9) | data formatting | bytes 524288
